TPU v7x, 32 devices: a whole 2x2x4 slice. The times are simulated.
32 devices in a mesh: member: 4 (over y, x), band: 8 (over z, core).
Axes of the slice: x: 2, y: 2, z: 4, core: 2. Of those that a mesh axis runs over, the one named last changes fastest.
Arguments:
- perturb: bfloat16 [80, 2, 16, 65536], P('member', None, None, 'band'), may hold values from -15 to 15
- control: float32 [2, 16, 65536], P(None, None, 'band'), may hold values from -6 to 6
- static_cov: float32 [2, 16, 16], replicated, may hold values from -1.5 to 1.5
- loc_table: bfloat16 [16, 256, 256], replicated, may hold values from -0.109375 to 0.109375
- pair_offset: int32 [256, 12], P('band'), may hold values from -6 to 6, as said below
- pair_table: int32 [256, 12], P('band'), may hold values from 0 to 15
- pair_count: int32 [256], P('band'), may hold values from 1 to 12, as said below
Outputs:
- increment: float32 [2, 16, 65536], P(None, 'member', 'band')
Inputs may be any that keep to these rules, and one draw needn't show every extreme that they name: `pair_offset`: the offsets of one block are distinct. `pair_count`: counting blocks in aligned runs of 32, the first 6 and the last 6 blocks of every run have all 12 slots live; so do all blocks of some runs, the first run among them.
All inputs are finite; a program needn't handle non-finite values.
Results may differ from a plain program's by a relative error of at most 0.0022.
Values may be sent and summed in bfloat16 or wider, within the bound.
A program may use at most 128 MiB of HBM per device.

v0:
```python
import jax
import jax.numpy as jnp
from jax import lax
from jax.sharding import PartitionSpec as P

HB = 6


def extended(cells, sides, width):
    for axis, dim in sides:
        count = lax.axis_size(axis)
        head = lax.slice_in_dim(cells, 0, width, axis=dim)
        tail = lax.slice_in_dim(cells, cells.shape[dim] - width, cells.shape[dim], axis=dim)
        cells = jnp.concatenate(
            [
                lax.ppermute(tail, axis, [(i, (i + 1) % count) for i in range(count)]),
                cells,
                lax.ppermute(head, axis, [((i + 1) % count, i) for i in range(count)]),
            ],
            axis=dim,
        )
    return cells


def localize(words, offsets, table_ids, counts, loc_table):
    rows, width = words.shape
    ntables = loc_table.shape[0]
    size = loc_table.shape[1]
    nblk = width // size
    blocks = jnp.transpose(words.reshape(rows, nblk, size), (1, 0, 2))
    padded = extended(blocks, (("band", 0),), HB)
    slot_ids = jnp.arange(offsets.shape[1], dtype=jnp.int32)
    live = slot_ids[None, :] < counts[:, None]
    table_hits = table_ids[:, :, None] == jnp.arange(ntables, dtype=jnp.int32)[None, None, :]

    def one_shift(shift, acc):
        window = lax.dynamic_slice_in_dim(padded, HB + shift, nblk, 0)
        match = (live & (offsets == shift))[:, :, None] & table_hits
        select = jnp.sum(match.astype(jnp.float32), axis=1).astype(jnp.bfloat16)
        tables = jnp.einsum(
            "bt,tij->bij", select, loc_table, preferred_element_type=jnp.float32
        ).astype(jnp.bfloat16)
        prod = jnp.einsum("bri,bij->brj", window, tables, preferred_element_type=jnp.float32)
        return acc + prod

    start_acc = jnp.zeros((nblk, rows, size), jnp.float32)
    result = lax.fori_loop(0, 2 * HB + 1, lambda step, acc: one_shift(step - HB, acc), start_acc)
    return jnp.transpose(result, (1, 0, 2)).reshape(rows, width)


def per_device(perturb, control, static_cov, loc_table, pair_offset, pair_table, pair_count):
    groups = lax.axis_size("member")
    levels = control.shape[1]
    share = levels // groups
    first = lax.axis_index("member") * share
    cov_mine = lax.dynamic_slice_in_dim(static_cov, first, share, 1)
    static = jnp.einsum("fml,flc->fmc", cov_mine, control, precision=lax.Precision.HIGHEST)
    total_members = perturb.shape[0] * groups
    owned = lax.all_to_all(perturb, "member", split_axis=2, concat_axis=0, tiled=True)
    control_mine = lax.dynamic_slice_in_dim(control, first, share, 1)
    words = (owned.astype(jnp.float32) * control_mine[None]).astype(jnp.bfloat16)
    kall, fields, depth, width = words.shape
    spread = localize(
        words.reshape(kall * fields * depth, width), pair_offset, pair_table, pair_count, loc_table
    )
    spread = spread.reshape(kall, fields, depth, width)
    ensemble = jnp.sum(owned.astype(jnp.float32) * spread, axis=0)
    return 0.5 * static + 0.5 * (ensemble / (total_members - 1))


def solution(mesh):
    return jax.shard_map(
        per_device,
        mesh=mesh,
        in_specs=(
            P("member", None, None, "band"),
            P(None, None, "band"),
            P(),
            P(),
            P("band", None),
            P("band", None),
            P("band"),
        ),
        out_specs=P(None, "member", "band"),
        check_vma=False,
    )
```

profile of v0, /device:TPU:0, one launch (start us, length us, event | category | flops | bytes accessed | tf_op | source)
XLA Modules:
  0.0 891.0 jit_solution(18180679911368565242)
XLA Ops:
  27.8 25.4 %mul.28 = f32[640,32,256]{2,1,0:T(8,128)} reshape(f32[80,2,4,8192]{3,2,1,0:T(4,128)} %mul.27) | data formatting | bytes 41943040 | tf_op jit(solution)/shard_map/mul | solution.py:61
  53.2 106.0 %all-to-all-done = bf16[20,2,16,8192]{3,0,1,2:T(8,128)(2,1)} async-done(((bf16[20,2,16,8192]{3,0,1,2:T(8,128)(2,1)}), bf16[20,2,16,8192]{3,0,1,2:T(8,128)(2,1)}, u32[]{:S(2)}, u32[]{:S(2)}) %all-to-all-start) | async-done | bytes 10485792 | tf_op jit(solution)/shard_map/all_to_all | solution.py:59
  159.1 16.5 %copy.57 = f32[20,2,4,4,8192]{4,3,1,0,2:T(4,128)} copy(bf16[20,2,4,4,8192]{4,0,1,3,2:T(8,128)(2,1)} %bitcast.6) | data formatting | bytes 31457280 | tf_op jit(solution)/shard_map/convert_element_type | solution.py:67
  175.7 25.3 %reshape.26 = f32[640,32,256]{2,1,0:T(8,128)} reshape(f32[4,20,2,4,8192]{4,3,2,1,0:T(4,128)} %bitcast.23) | data formatting | bytes 41943040 | tf_op jit(solution)/shard_map/convert_element_type | solution.py:67
  201.0 14.0 %fusion.14 = bf16[32,640,256]{2,0,1:T(8,128)(2,1)S(1)} fusion(f32[640,32,256]{2,1,0:T(8,128)} %reshape.26, f32[640,32,256]{2,1,0:T(8,128)} %mul.28), kind=kLoop, calls=%fused_computation.19 | loop fusion | flops 10485760 | bytes 52428800 | tf_op jit(solution)/shard_map/transpose | solution.py:30
  229.8 17.5 %copy.41 = f32[20,2,4,4,8192]{4,3,1,0,2:T(4,128)} copy(bf16[20,2,4,4,8192]{4,0,1,3,2:T(8,128)(2,1)} %bitcast.6) | data formatting | bytes 31457280 | tf_op jit(solution)/shard_map/convert_element_type | solution.py:67
  247.3 17.5 %collective-permute-done = bf16[6,640,256]{2,1,0:T(8,128)(2,1)} collective-permute-done((bf16[6,640,256]{2,1,0:T(8,128)(2,1)}, bf16[6,640,256]{2,1,0:T(8,128)(2,1)}, u32[]{:S(2)}, u32[]{:S(2)}) %collective-permute-start) | collective-permute-done | bytes 1966112 | tf_op jit(solution)/shard_map/ppermute | solution.py:16
  280.9 544.5 %while.18 = (s32[]{:T(128)}, f32[32,640,256]{2,1,0:T(8,128)}, bf16[44,640,256]{2,0,1:T(8,128)(2,1)}, s32[32,12]{0,1:T(8,128)S(1)}, bf16[16,256,256]{2,0,1:T(8,12...) while((s32[]{:T(128)}, f32[32,640,256]{2,1,0:T(8,128)}, ...), condition=%wide.region_2.0_spmd.clone, body=%wide.region_0.0_spmd.clone.sunk | while | flops 2764071424 | bytes 83892224 | solution.py:47
  297.6 21.5 %select_add_fusion.2 = f32[32,640,256]{2,1,0:T(8,128)} fusion(f32[32,640,256]{2,1,0:T(8,128)} %get-tuple-element.364, pred[]{:T(512)S(6)} %compare.3, bf16[32,640,256]{2,0,1:T(8,128)(2,1)} %constant_dynamic-slice_fusion.3, bf16[32,256,256]{2,0,1:T(8,128)(2,1)} %convolution_convert_fusion.2), kind=kOutput, calls=%fused_computation.2.clone.1 | convolution fusion | flops 2694840320 | bytes 56623104 | tf_op jit(solution)/shard_map/while/body/eval_jaxpr/bri,bij->brj/dot_general | solution.py:43
  335.4 25.8 %select_add_fusion.2 = f32[32,640,256]{2,1,0:T(8,128)} fusion(f32[32,640,256]{2,1,0:T(8,128)} %get-tuple-element.364, pred[]{:T(512)S(6)} %compare.3, bf16[32,640,256]{2,0,1:T(8,128)(2,1)} %constant_dynamic-slice_fusion.3, bf16[32,256,256]{2,0,1:T(8,128)(2,1)} %convolution_convert_fusion.2), kind=kOutput, calls=%fused_computation.2.clone.1 | convolution fusion | flops 2694840320 | bytes 56623104 | tf_op jit(solution)/shard_map/while/body/eval_jaxpr/bri,bij->brj/dot_general | solution.py:43
  377.6 25.8 %select_add_fusion.2 = f32[32,640,256]{2,1,0:T(8,128)} fusion(f32[32,640,256]{2,1,0:T(8,128)} %get-tuple-element.364, pred[]{:T(512)S(6)} %compare.3, bf16[32,640,256]{2,0,1:T(8,128)(2,1)} %constant_dynamic-slice_fusion.3, bf16[32,256,256]{2,0,1:T(8,128)(2,1)} %convolution_convert_fusion.2), kind=kOutput, calls=%fused_computation.2.clone.1 | convolution fusion | flops 2694840320 | bytes 56623104 | tf_op jit(solution)/shard_map/while/body/eval_jaxpr/bri,bij->brj/dot_general | solution.py:43
  419.8 25.8 %select_add_fusion.2 = f32[32,640,256]{2,1,0:T(8,128)} fusion(f32[32,640,256]{2,1,0:T(8,128)} %get-tuple-element.364, pred[]{:T(512)S(6)} %compare.3, bf16[32,640,256]{2,0,1:T(8,128)(2,1)} %constant_dynamic-slice_fusion.3, bf16[32,256,256]{2,0,1:T(8,128)(2,1)} %convolution_convert_fusion.2), kind=kOutput, calls=%fused_computation.2.clone.1 | convolution fusion | flops 2694840320 | bytes 56623104 | tf_op jit(solution)/shard_map/while/body/eval_jaxpr/bri,bij->brj/dot_general | solution.py:43
  462.0 25.8 %select_add_fusion.2 = f32[32,640,256]{2,1,0:T(8,128)} fusion(f32[32,640,256]{2,1,0:T(8,128)} %get-tuple-element.364, pred[]{:T(512)S(6)} %compare.3, bf16[32,640,256]{2,0,1:T(8,128)(2,1)} %constant_dynamic-slice_fusion.3, bf16[32,256,256]{2,0,1:T(8,128)(2,1)} %convolution_convert_fusion.2), kind=kOutput, calls=%fused_computation.2.clone.1 | convolution fusion | flops 2694840320 | bytes 56623104 | tf_op jit(solution)/shard_map/while/body/eval_jaxpr/bri,bij->brj/dot_general | solution.py:43
  504.2 25.8 %select_add_fusion.2 = f32[32,640,256]{2,1,0:T(8,128)} fusion(f32[32,640,256]{2,1,0:T(8,128)} %get-tuple-element.364, pred[]{:T(512)S(6)} %compare.3, bf16[32,640,256]{2,0,1:T(8,128)(2,1)} %constant_dynamic-slice_fusion.3, bf16[32,256,256]{2,0,1:T(8,128)(2,1)} %convolution_convert_fusion.2), kind=kOutput, calls=%fused_computation.2.clone.1 | convolution fusion | flops 2694840320 | bytes 56623104 | tf_op jit(solution)/shard_map/while/body/eval_jaxpr/bri,bij->brj/dot_general | solution.py:43
  546.4 25.8 %select_add_fusion.2 = f32[32,640,256]{2,1,0:T(8,128)} fusion(f32[32,640,256]{2,1,0:T(8,128)} %get-tuple-element.364, pred[]{:T(512)S(6)} %compare.3, bf16[32,640,256]{2,0,1:T(8,128)(2,1)} %constant_dynamic-slice_fusion.3, bf16[32,256,256]{2,0,1:T(8,128)(2,1)} %convolution_convert_fusion.2), kind=kOutput, calls=%fused_computation.2.clone.1 | convolution fusion | flops 2694840320 | bytes 56623104 | tf_op jit(solution)/shard_map/while/body/eval_jaxpr/bri,bij->brj/dot_general | solution.py:43
  588.6 25.8 %select_add_fusion.2 = f32[32,640,256]{2,1,0:T(8,128)} fusion(f32[32,640,256]{2,1,0:T(8,128)} %get-tuple-element.364, pred[]{:T(512)S(6)} %compare.3, bf16[32,640,256]{2,0,1:T(8,128)(2,1)} %constant_dynamic-slice_fusion.3, bf16[32,256,256]{2,0,1:T(8,128)(2,1)} %convolution_convert_fusion.2), kind=kOutput, calls=%fused_computation.2.clone.1 | convolution fusion | flops 2694840320 | bytes 56623104 | tf_op jit(solution)/shard_map/while/body/eval_jaxpr/bri,bij->brj/dot_general | solution.py:43
  630.8 25.8 %select_add_fusion.2 = f32[32,640,256]{2,1,0:T(8,128)} fusion(f32[32,640,256]{2,1,0:T(8,128)} %get-tuple-element.364, pred[]{:T(512)S(6)} %compare.3, bf16[32,640,256]{2,0,1:T(8,128)(2,1)} %constant_dynamic-slice_fusion.3, bf16[32,256,256]{2,0,1:T(8,128)(2,1)} %convolution_convert_fusion.2), kind=kOutput, calls=%fused_computation.2.clone.1 | convolution fusion | flops 2694840320 | bytes 56623104 | tf_op jit(solution)/shard_map/while/body/eval_jaxpr/bri,bij->brj/dot_general | solution.py:43
  673.0 25.8 %select_add_fusion.2 = f32[32,640,256]{2,1,0:T(8,128)} fusion(f32[32,640,256]{2,1,0:T(8,128)} %get-tuple-element.364, pred[]{:T(512)S(6)} %compare.3, bf16[32,640,256]{2,0,1:T(8,128)(2,1)} %constant_dynamic-slice_fusion.3, bf16[32,256,256]{2,0,1:T(8,128)(2,1)} %convolution_convert_fusion.2), kind=kOutput, calls=%fused_computation.2.clone.1 | convolution fusion | flops 2694840320 | bytes 56623104 | tf_op jit(solution)/shard_map/while/body/eval_jaxpr/bri,bij->brj/dot_general | solution.py:43
  715.2 25.8 %select_add_fusion.2 = f32[32,640,256]{2,1,0:T(8,128)} fusion(f32[32,640,256]{2,1,0:T(8,128)} %get-tuple-element.364, pred[]{:T(512)S(6)} %compare.3, bf16[32,640,256]{2,0,1:T(8,128)(2,1)} %constant_dynamic-slice_fusion.3, bf16[32,256,256]{2,0,1:T(8,128)(2,1)} %convolution_convert_fusion.2), kind=kOutput, calls=%fused_computation.2.clone.1 | convolution fusion | flops 2694840320 | bytes 56623104 | tf_op jit(solution)/shard_map/while/body/eval_jaxpr/bri,bij->brj/dot_general | solution.py:43
  757.4 25.8 %select_add_fusion.2 = f32[32,640,256]{2,1,0:T(8,128)} fusion(f32[32,640,256]{2,1,0:T(8,128)} %get-tuple-element.364, pred[]{:T(512)S(6)} %compare.3, bf16[32,640,256]{2,0,1:T(8,128)(2,1)} %constant_dynamic-slice_fusion.3, bf16[32,256,256]{2,0,1:T(8,128)(2,1)} %convolution_convert_fusion.2), kind=kOutput, calls=%fused_computation.2.clone.1 | convolution fusion | flops 2694840320 | bytes 56623104 | tf_op jit(solution)/shard_map/while/body/eval_jaxpr/bri,bij->brj/dot_general | solution.py:43
  799.6 25.8 %select_add_fusion.2 = f32[32,640,256]{2,1,0:T(8,128)} fusion(f32[32,640,256]{2,1,0:T(8,128)} %get-tuple-element.364, pred[]{:T(512)S(6)} %compare.3, bf16[32,640,256]{2,0,1:T(8,128)(2,1)} %constant_dynamic-slice_fusion.3, bf16[32,256,256]{2,0,1:T(8,128)(2,1)} %convolution_convert_fusion.2), kind=kOutput, calls=%fused_computation.2.clone.1 | convolution fusion | flops 2694840320 | bytes 56623104 | tf_op jit(solution)/shard_map/while/body/eval_jaxpr/bri,bij->brj/dot_general | solution.py:43
  825.5 21.3 %copy.48 = f32[640,32,256]{2,1,0:T(8,128)} copy(f32[640,32,256]{2,0,1:T(8,128)} %bitcast.22) | data formatting | bytes 41943040 | tf_op jit(solution)/shard_map/transpose | solution.py:48
  846.8 25.7 %reshape_reshape.4 = f32[80,2,4,8192]{3,2,1,0:T(4,128)} reshape(f32[640,32,256]{2,1,0:T(8,128)} %copy.48) | data formatting | bytes 41943040 | tf_op jit(solution)/shard_map/reshape;reshape | solution.py:66
  872.5 16.4 %fusion.13 = f32[2,4,8192]{2,1,0:T(4,128)S(1)} fusion(f32[80,2,4,8192]{3,2,1,0:T(4,128)} %reshape_reshape.4, f32[20,2,4,4,8192]{4,3,1,0,2:T(4,128)} %copy.41), kind=kLoop, calls=%fused_computation.16 | loop fusion | flops 10420224 | bytes 42205184 | tf_op jit(solution)/shard_map/reduce_sum | solution.py:67
  (85 shorter events, 273.4 us)
Async XLA Ops:
  0.0 20.3 %copy-start = (f32[2,16,8192]{2,1,0:T(8,128)S(1)}, f32[2,16,8192]{2,1,0:T(8,128)}, u32[]{:S(2)}) copy-start(f32[2,16,8192]{2,1,0:T(8,128)} %param.10) | copy-start | bytes 3145732
  14.0 145.1 %all-to-all-start = ((bf16[20,2,16,8192]{3,0,1,2:T(8,128)(2,1)}), bf16[20,2,16,8192]{3,0,1,2:T(8,128)(2,1)}, u32[]{:S(2)}, u32[]{:S(2)}) async-start(bf16[20,2,16,8192]{3,0,1,2:T(8,128)(2,1)} %copy.40), calls=%async_computation | async-start | bytes 25165824 | tf_op jit(solution)/shard_map/all_to_all | solution.py:59
  215.0 3.9 copy-start.1
  221.6 43.2 %collective-permute-start = (bf16[6,640,256]{2,1,0:T(8,128)(2,1)}, bf16[6,640,256]{2,1,0:T(8,128)(2,1)}, u32[]{:S(2)}, u32[]{:S(2)}) collective-permute-start(bf16[6,640,256]{2,1,0:T(8,128)(2,1)} %copy.42), channel_id=1, source_target_pairs={{0,1},{1,2},{2,3},{3,4},{4,5},{5,6},{6,7},{7,0},{8,9},{9,10},{10,1... | collective-permute-start | bytes 5898248 | tf_op jit(solution)/shard_map/ppermute | solution.py:16
  223.3 44.2 %collective-permute-start.1 = (bf16[6,640,256]{2,1,0:T(8,128)(2,1)}, bf16[6,640,256]{2,1,0:T(8,128)(2,1)}, u32[]{:S(2)}, u32[]{:S(2)}) collective-permute-start(bf16[6,640,256]{2,1,0:T(8,128)(2,1)} %copy.43), channel_id=1, source_target_pairs={{1,0},{2,1},{3,2},{4,3},{5,4},{6,5},{7,6},{0,7},{9,8},{10,9},{11,1... | collective-permute-start | bytes 5898248 | tf_op jit(solution)/shard_map/ppermute | solution.py:18
  226.9 43.3 %slice-start = ((s8[10485760]{0:T(1024)(128)(4,1)}), s8[4194304]{0:T(1024)(128)(4,1)S(1)}, s32[]{:S(2)}) async-start(s8[10485760]{0:T(1024)(128)(4,1)} %bitcast.24), calls=%async_computation.1 | async-start | bytes 8388608
  229.8 40.4 %slice-start.1 = ((s8[10485760]{0:T(1024)(128)(4,1)}), s8[4194304]{0:T(1024)(128)(4,1)S(1)}, s32[]{:S(2)}) async-start(s8[10485760]{0:T(1024)(128)(4,1)} %bitcast.24), calls=%async_computation.2 | async-start | bytes 8388608
  229.8 40.4 %slice-start.2 = ((s8[10485760]{0:T(1024)(128)(4,1)}), s8[2097152]{0:T(1024)(128)(4,1)S(1)}, s32[]{:S(2)}) async-start(s8[10485760]{0:T(1024)(128)(4,1)} %bitcast.24), calls=%async_computation.3 | async-start | bytes 4194304
  270.2 10.7 %copy-start.2 = (s32[32,12]{0,1:T(8,128)S(1)}, s32[32,12]{0,1:T(8,128)}, u32[]{:S(2)}) copy-start(s32[32,12]{0,1:T(8,128)} %param.14) | copy-start | bytes 4612
  270.2 10.7 %copy-start.3 = (s32[32,12]{0,1:T(8,128)S(1)}, s32[32,12]{0,1:T(8,128)}, u32[]{:S(2)}) copy-start(s32[32,12]{0,1:T(8,128)} %param.13) | copy-start | bytes 4612
  270.2 10.7 %copy-start.4 = (s32[32]{0:T(128)S(1)}, s32[32]{0:T(128)}, u32[]{:S(2)}) copy-start(s32[32]{0:T(128)} %param.15) | copy-start | bytes 388
where the time goes:
time: 896 us; the launch traced here: 891 us
  matrix products  376 us (42%)
  local copies, waits for them, and re-layouts  339 us (38%)
  waiting for transfers between devices  123 us (14%)
  other arithmetic  41.6 us (5%)
  starting transfers between devices  9.85 us (1%)
    dot_general x13, matrix products, one_shift(): jnp.einsum('bri,bij->brj', window, tables, preferred_element_type=jnp.flo...  331 us
    dynamic_slice x13, local copies, waits for them, and re-layouts, one_shift(): window = lax.dynamic_slice_in_dim(padded, HB + shift, nblk, 0)  170 us
    all_to_all x1, waiting for transfers between devices, per_device(): lax.all_to_all(perturb, 'member', split_axis=2, concat_axis=0, tiled=True)  106 us
    convert_element_type x3, local copies, waits for them, and re-layouts, per_device(): ensemble = jnp.sum(owned.astype(jnp.float32) * spread, axis=0)  59.4 us
    dot_general x13, matrix products, one_shift(): jnp.einsum('bt,tij->bij', select, loc_table, preferred_element_type=jnp.f...  42.7 us
    mul x2, local copies, waits for them, and re-layouts, per_device(): owned.astype(jnp.float32) * control_mine[None]  32.8 us
    another operation x1, local copies, waits for them, and re-layouts, per_device(): spread = spread.reshape(kall, fields, depth, width)  25.7 us
    transpose x1, local copies, waits for them, and re-layouts, localize(): return jnp.transpose(result, (1, 0, 2)).reshape(rows, width)  21.3 us
  transfers between devices with their start and end apart: 3, of which 2 were waited for; matrix products, arithmetic and copies ran while one was open for 6% of the time, Pallas kernels for 0%

commit v1 on v0

v1 whole, which is shorter than its diff:
```python
import functools

import jax
import jax.numpy as jnp
from jax import lax
from jax.experimental import pallas as pl
from jax.experimental.pallas import tpu as pltpu
from jax.sharding import PartitionSpec as P

HB = 6
HALF = HB // 2
MESH = pl.DeviceIdType.MESH


def kernel(
    groups, bands, nblk, size, nslots, fields, levels, ntab, scale,
    info_s, info_h, perturb_h, control_h, table_h, cov_ref,
    out_ref,
    own, halo, words, tables, ctl, ctl_halo, info_halo, info_side,
    part_in, recv_in, part_edge, recv_edge, away, back,
    own_sem, misc_sem, side_sem, hsend, hrecv, asend, arecv, rsend, rrecv,
):
    rows = perturb_h.shape[0]
    depth = fields * levels
    share = levels // groups
    last = nblk + 2 * HALF
    me = lax.axis_index("member")
    mine = lax.axis_index("band")
    right = lax.rem(mine + 1, bands)
    left = lax.rem(mine + bands - 1, bands)

    barrier = pltpu.get_barrier_semaphore()
    for there in (left, right):
        pl.semaphore_signal(barrier, inc=1, device_id={"band": there}, device_id_type=MESH)
    for d in range(1, groups):
        pl.semaphore_signal(
            barrier, inc=1, device_id={"member": lax.rem(me + d, groups)}, device_id_type=MESH
        )

    def load(b):
        return pltpu.make_async_copy(
            perturb_h.at[:, pl.ds(pl.multiple_of(b * size, size), size)], own.at[b], own_sem.at[b]
        )

    def start_load(b, carry):
        load(b).start()
        return carry

    loads = [
        pltpu.make_async_copy(control_h, ctl, misc_sem.at[0]),
        pltpu.make_async_copy(table_h, tables.at[pl.ds(0, ntab)], misc_sem.at[1]),
    ]
    for copy in loads:
        copy.start()
    lax.fori_loop(0, nblk, start_load, 0)
    pl.semaphore_wait(barrier, 2 + groups - 1)

    halo_copies = []
    for side, there, first, row in ((0, right, nblk - HALF, nblk - 8), (1, left, 0, 0)):
        for n, (src, dst) in enumerate(
            [
                (info_h.at[pl.ds(row, 8)], info_halo.at[side]),
                (control_h.at[:, pl.ds(first * size, HALF * size)], ctl_halo.at[side]),
            ]
            + [
                (perturb_h.at[:, pl.ds((first + i) * size, size)], halo.at[side, i])
                for i in range(HALF)
            ]
        ):
            halo_copies.append(
                pltpu.make_async_remote_copy(
                    src_ref=src, dst_ref=dst, send_sem=hsend.at[side, n], recv_sem=hrecv.at[side, n],
                    device_id={"band": there}, device_id_type=MESH,
                )
            )
    for copy in halo_copies:
        copy.start()

    def word_of(block, weights):
        cells = block.astype(jnp.float32).reshape(rows // depth, depth, size) * weights[None]
        return cells.astype(jnp.bfloat16).reshape(rows, size)

    tables[ntab] = jnp.zeros((size, size), jnp.bfloat16)
    for i in range(HALF):
        words[i] = jnp.zeros((rows, size), jnp.bfloat16)
        words[nblk + HALF + i] = jnp.zeros((rows, size), jnp.bfloat16)
    for copy in loads:
        copy.wait()

    def make_words(b, carry):
        load(b).wait()
        words[b + HALF] = word_of(own[b], ctl[:, pl.ds(pl.multiple_of(b * size, size), size)])
        return carry

    lax.fori_loop(0, nblk, make_words, 0)

    def localize(cells, picks):
        lhs = jnp.concatenate([words[c] for c, _ in picks], axis=1)
        rhs = jnp.concatenate([tables[t] for _, t in picks], axis=0)
        spread = jnp.dot(lhs, rhs, preferred_element_type=jnp.float32)
        terms = cells.astype(jnp.float32) * spread
        return jnp.sum(terms.reshape(rows // depth, depth, size), axis=0)

    def put(dst, total):
        for m in range(groups):
            for f in range(fields):
                at = f * levels + m * share
                dst(m, slice(f * share, (f + 1) * share), total[at:at + share])

    def interior(n, carry):
        b = n + HB
        picks = [
            (b + HALF + info_s[b, s], info_s[b, nslots + s]) for s in range(nslots)
        ]
        cols = pl.ds(pl.multiple_of(n * size, size), size)

        def dst(m, at, value):
            part_in[m, at, cols] = value

        put(dst, localize(own[b], picks))
        return carry

    lax.fori_loop(0, nblk - 2 * HB, interior, 0)

    def to_members(src, dst, n):
        copies = []
        for d in range(1, groups):
            there = lax.rem(me + d, groups)
            copies.append(
                pltpu.make_async_remote_copy(
                    src_ref=src.at[there], dst_ref=dst.at[d - 1],
                    send_sem=rsend.at[n, d - 1], recv_sem=rrecv.at[n, d - 1],
                    device_id={"member": there}, device_id_type=MESH,
                )
            )
        for copy in copies:
            copy.start()
        return copies

    sums = to_members(part_in, recv_in, 0)

    out_ref[...] = 0.5 * jnp.dot(
        cov_ref[...], ctl[...], precision=lax.Precision.HIGHEST, preferred_element_type=jnp.float32
    )

    for copy in halo_copies:
        copy.wait()
    sides = [
        pltpu.make_async_copy(info_halo.at[side], info_side.at[side], side_sem.at[side])
        for side in range(2)
    ]
    for copy in sides:
        copy.start()
    for side in range(2):
        for i in range(HALF):
            words[side * (nblk + HALF) + i] = word_of(
                halo[side, i], ctl_halo[side, :, i * size:(i + 1) * size]
            )
    for copy in sides:
        copy.wait()

    for side in range(2):
        for i in range(HALF):
            row = 8 - HALF + i if side == 0 else i
            b = i if side == 0 else nblk + HALF + i
            partners = range(2 * HALF, 2 * HALF + i + 1) if side == 0 else range(
                b - HB, nblk
            )
            picks = []
            for c in partners:
                t = jnp.int32(ntab)
                for s in range(nslots):
                    hit = info_side[side, row, s] == c - b
                    t = jnp.where(hit, info_side[side, row, nslots + s], t)
                picks.append((c, t))
            total = localize(halo[side, i], picks)

            def dst(m, at, value):
                away[side, m, at, i * size:(i + 1) * size] = value

            put(dst, total)
    away_copies = [
        pltpu.make_async_remote_copy(
            src_ref=away.at[side], dst_ref=back.at[1 - side],
            send_sem=asend.at[side], recv_sem=arecv.at[side],
            device_id={"band": there}, device_id_type=MESH,
        )
        for side, there in ((0, left), (1, right))
    ]
    for copy in away_copies:
        copy.start()

    for side in range(2):
        def edge(n, carry):
            b = n + side * (nblk - HB)
            picks = []
            for s in range(nslots):
                c = b + HALF + info_s[b, s]
                held = (c >= 0) & (c < last)
                picks.append(
                    (jnp.clip(c, 0, last - 1), jnp.where(held, info_s[b, nslots + s], ntab))
                )
            cols = pl.ds(pl.multiple_of(n * size, size), size)

            def dst(m, at, value):
                part_edge[side, m, at, cols] = value

            put(dst, localize(own[b], picks))
            return carry

        lax.fori_loop(0, HB, edge, 0)
        if side == 0:
            for copy in away_copies:
                copy.wait()
        near = pl.ds(side * HALF * size, HALF * size)
        part_edge[side, :, :, near] = part_edge[side, :, :, near] + back[side]
        sums = sums + to_members(part_edge.at[side], recv_edge.at[side], 1 + side)

    for copy in sums:
        copy.wait()

    def finish(first, width, own_part, others):
        total = own_part
        for d in range(groups - 1):
            total = total + others[d]
        cols = slice(first * size, (first + width) * size)
        out_ref[:, cols] = out_ref[:, cols] + 0.5 * (total / scale)

    finish(HB, nblk - 2 * HB, part_in[me], recv_in)
    for side in range(2):
        finish(side * (nblk - HB), HB, part_edge[side, me], recv_edge.at[side])


def per_device(perturb, control, static_cov, loc_table, pair_offset, pair_table, pair_count):
    groups = lax.axis_size("member")
    bands = lax.axis_size("band")
    members, fields, levels, width = perturb.shape
    ntab, size = loc_table.shape[:2]
    nblk, nslots = pair_offset.shape
    share = levels // groups
    rows = members * fields * levels
    depth = fields * levels

    live = jnp.arange(nslots, dtype=jnp.int32)[None, :] < pair_count[:, None]
    info = jnp.concatenate(
        [jnp.where(live, pair_offset, 0), jnp.where(live, pair_table, ntab)], axis=1
    )
    info = jnp.pad(info, ((0, 0), (0, 128 - 2 * nslots)))
    first = lax.axis_index("member") * share
    cov_mine = lax.dynamic_slice_in_dim(static_cov, first, share, 1)
    cov = (cov_mine[:, :, None, :] * jnp.eye(fields, dtype=jnp.float32)[:, None, :, None]).reshape(
        fields * share, depth
    )

    out_rows = fields * share
    f32, bf16 = jnp.float32, jnp.bfloat16
    any_spec = pl.BlockSpec(memory_space=pl.ANY)
    dma = pltpu.SemaphoreType.DMA
    pairs = nblk * nslots
    out = pl.pallas_call(
        functools.partial(
            kernel, groups, bands, nblk, size, nslots, fields, levels, ntab, members * groups - 1
        ),
        out_shape=jax.ShapeDtypeStruct((out_rows, width), f32),
        in_specs=[
            pl.BlockSpec(memory_space=pltpu.SMEM), any_spec, any_spec, any_spec, any_spec,
            pl.BlockSpec(memory_space=pltpu.VMEM),
        ],
        out_specs=pl.BlockSpec(memory_space=pltpu.VMEM),
        scratch_shapes=[
            pltpu.VMEM((nblk, rows, size), bf16),
            pltpu.VMEM((2, HALF, rows, size), bf16),
            pltpu.VMEM((nblk + 2 * HALF, rows, size), bf16),
            pltpu.VMEM((ntab + 1, size, size), bf16),
            pltpu.VMEM((depth, width), f32),
            pltpu.VMEM((2, depth, HALF * size), f32),
            pltpu.VMEM((2, 8, 128), jnp.int32),
            pltpu.SMEM((2, 8, 128), jnp.int32),
            pltpu.VMEM((groups, out_rows, width - 2 * HB * size), f32),
            pltpu.VMEM((groups - 1, out_rows, width - 2 * HB * size), f32),
            pltpu.VMEM((2, groups, out_rows, HB * size), f32),
            pltpu.VMEM((2, groups - 1, out_rows, HB * size), f32),
            pltpu.VMEM((2, groups, out_rows, HALF * size), f32),
            pltpu.VMEM((2, groups, out_rows, HALF * size), f32),
            dma((nblk,)), dma((2,)), dma((2,)),
            dma((2, 2 + HALF)), dma((2, 2 + HALF)),
            dma((2,)), dma((2,)),
            dma((3, groups - 1)), dma((3, groups - 1)),
        ],
        compiler_params=pltpu.CompilerParams(
            collective_id=0, has_side_effects=True, vmem_limit_bytes=56 * 1024 * 1024
        ),
        cost_estimate=pl.CostEstimate(
            flops=2 * pairs * rows * size * size, bytes_accessed=2 * rows * width, transcendentals=0
        ),
    )(info, info, perturb.reshape(rows, width), control.reshape(depth, width), loc_table, cov)
    return out.reshape(fields, share, width)


def solution(mesh):
    return jax.shard_map(
        per_device,
        mesh=mesh,
        in_specs=(
            P("member", None, None, "band"),
            P(None, None, "band"),
            P(),
            P(),
            P("band", None),
            P("band", None),
            P("band"),
        ),
        out_specs=P(None, "member", "band"),
        check_vma=False,
    )
```

time: 896 us -> 61.1 us (0.07)
  matrix products: 376 us -> 0 us
  local copies, waits for them, and re-layouts: 339 us -> 5.28 us
  waiting for transfers between devices: 123 us -> 0 us
  Pallas kernels: 0 us -> 54.4 us
  other arithmetic: 41.6 us -> 0.88 us
  starting transfers between devices: 9.85 us -> 0 us
    dot_general x27 -> x0, matrix products: 376 us -> none  [the longest x13 331 us: one_shift(): jnp.einsum('bri,bij->brj', window, tables, preferred_element_type=jnp.flo...]
    dynamic_slice x14 -> x1, local copies, waits for them, and re-layouts: 170 us -> 0.01 us  [per_device(): cov_mine = lax.dynamic_slice_in_dim(static_cov, first, share, 1)]
    all_to_all x1 -> x0, waiting for transfers between devices: 106 us -> none  [per_device(): lax.all_to_all(perturb, 'member', split_axis=2, concat_axis=0, tiled=True)]
    convert_element_type x3 -> x0, local copies, waits for them, and re-layouts: 59.4 us -> none  [per_device(): ensemble = jnp.sum(owned.astype(jnp.float32) * spread, axis=0)]
    pallas_call x0 -> x1, Pallas kernels: none -> 54.4 us  [per_device(): pl.pallas_call(functools.partial(kernel, groups, bands, nblk, size, nslot...]
    mul x2 -> x1, local copies, waits for them, and re-layouts: 32.8 us -> 0.67 us  [per_device(): cov_mine[:, :, None, :]]
    another operation x1 -> x0, local copies, waits for them, and re-layouts: 25.7 us -> none  [per_device(): spread = spread.reshape(kall, fields, depth, width)]
    transpose x1 -> x0, local copies, waits for them, and re-layouts: 21.3 us -> none  [localize(): return jnp.transpose(result, (1, 0, 2)).reshape(rows, width)]
  transfers between devices with their start and end apart: 3 -> 0, of which waited for: 2 -> 0; matrix products, arithmetic and copies ran while one was open for 6% -> 0% of each run, Pallas kernels for 0% -> 0%
where the time goes in v1:
time: 61.1 us; the launch traced here: 60.6 us
  Pallas kernels  54.4 us (89%)
  local copies, waits for them, and re-layouts  5.28 us (9%)
  other arithmetic  0.88 us (1%)
    pallas_call x1, Pallas kernels, per_device(): pl.pallas_call(functools.partial(kernel, groups, bands, nblk, size, nslot...  54.4 us
    unnamed x4, local copies, waits for them, and re-layouts  2.26 us
    reshape x1, local copies, waits for them, and re-layouts, per_device(): return out.reshape(fields, share, width)  1.73 us

profile of v1, /device:TPU:0, one launch (start us, length us, event | category | flops | bytes accessed | tf_op | source)
XLA Modules:
  0.0 60.6 jit_solution(15125812104247672634)
XLA Ops:
  0.0 0.0 copy-start
  0.0 0.7 %copy-done = f32[2,16,16]{2,1,0:T(8,128)S(1)} copy-done((f32[2,16,16]{2,1,0:T(8,128)S(1)}, f32[2,16,16]{2,1,0:T(8,128)}, u32[]{:S(2)}) %copy-start) | copy-done | bytes 2072
  0.7 0.1 broadcast_multiply_fusion
  0.8 0.7 %mul.24.cov_ref = f32[8,32]{1,0:T(8,128)} reshape(f32[2,4,2,16]{3,2,1,0:T(2,128)S(1)} %broadcast_multiply_fusion) | data formatting | bytes 2048 | tf_op jit(solution)/shard_map/mul | solution.py:251
  1.5 0.8 %copy.8 = s32[32,12]{1,0:T(8,128)S(1)} copy(s32[32,12]{0,1:T(8,128)} %param.11) | data formatting | bytes 3072 | tf_op args[4]
  2.3 0.8 %copy.9 = s32[32,12]{1,0:T(8,128)S(1)} copy(s32[32,12]{0,1:T(8,128)} %param.12) | data formatting | bytes 3072 | tf_op args[5]
  3.0 0.7 %fusion.1 = (s32[32,12]{1,0:T(8,128)S(1)}, s32[32,12]{1,0:T(8,128)S(1)}) fusion(s32[32,12]{1,0:T(8,128)S(1)} %copy.8, s32[32]{0:T(128)} %param.13, s32[32,12]{1,0:T(8,128)S(1)} %copy.9), kind=kLoop, calls=%fused_computation.3 | loop fusion | flops 1152 | bytes 6272 | tf_op jit(solution)/shard_map/jit(_where)/select_n | solution.py:246
  3.8 0.1 pad_add_fusion
  3.8 0.6 %pad.4.info_s.info_h = s32[32,128]{1,0:T(8,128)} pad(s32[32,24]{1,0:T(8,128)S(1)} %pad_add_fusion, s32[]{:T(128)} %constant.4.clone.1), padding=0_0x0_104 | pad | bytes 19460 | tf_op jit(solution)/shard_map/jit(_pad)/pad | solution.py:248
  4.4 54.4 %shard_map.73 = f32[8,8192]{1,0:T(8,128)} custom-call(s32[32,128]{1,0:T(8,128)} %pad.4.info_s.info_h, s32[32,128]{1,0:T(8,128)} %pad.4.info_s.info_h, bf16[640,8192]{1,0:T(8,128)(2,1)} %bitcast.2, f32[32,8192]{1,0:T(8,128)} %bitcast.3, bf16[16,256,256]{2,1,0:T(8,128)(2,1)} %table_h.1, f32[8,32]{1,0:T(8,128)} %mul.24.cov_ref), custom_call_target="tpu_custom_call" | custom-call | flops 32212254720 | bytes 10485760 | tf_op jit(solution)/shard_map/pallas_call | solution.py:260
  58.9 1.7 %reshape.25 = f32[2,4,8192]{2,1,0:T(4,128)} reshape(f32[8,8192]{1,0:T(8,128)} %shard_map.73) | data formatting | bytes 524288 | tf_op jit(solution)/shard_map/reshape | solution.py:297
  (2 shorter events, 0.0 us)
Async XLA Ops:
  0.0 0.7 %copy-start = (f32[2,16,16]{2,1,0:T(8,128)S(1)}, f32[2,16,16]{2,1,0:T(8,128)}, u32[]{:S(2)}) copy-start(f32[2,16,16]{2,1,0:T(8,128)} %param.9) | copy-start | bytes 6148

commit v2 on v1

--- a/solution.py
+++ b/solution.py
@@ -14,9 +14,10 @@
 
 def kernel(
     groups, bands, nblk, size, nslots, fields, levels, ntab, scale,
-    info_s, info_h, perturb_h, control_h, table_h, cov_ref,
+    off_s, tab_s, cnt_s, off_h, tab_h, cnt_h, perturb_h, control_h, table_h, cov_ref,
     out_ref,
-    own, halo, words, tables, ctl, ctl_halo, info_halo, info_side,
+    own, halo, words, tables, ctl, ctl_halo,
+    off_halo, tab_halo, cnt_halo, off_side, tab_side, cnt_side,
     part_in, recv_in, part_edge, recv_edge, away, back,
     own_sem, misc_sem, side_sem, hsend, hrecv, asend, arecv, rsend, rrecv,
 ):
@@ -56,10 +57,12 @@
     pl.semaphore_wait(barrier, 2 + groups - 1)
 
     halo_copies = []
-    for side, there, first, row in ((0, right, nblk - HALF, nblk - 8), (1, left, 0, 0)):
+    for side, there, first in ((0, right, nblk - HALF), (1, left, 0)):
         for n, (src, dst) in enumerate(
             [
-                (info_h.at[pl.ds(row, 8)], info_halo.at[side]),
+                (off_h, off_halo.at[side]),
+                (tab_h, tab_halo.at[side]),
+                (cnt_h, cnt_halo.at[side]),
                 (control_h.at[:, pl.ds(first * size, HALF * size)], ctl_halo.at[side]),
             ]
             + [
@@ -95,9 +98,10 @@
     lax.fori_loop(0, nblk, make_words, 0)
 
     def localize(cells, picks):
-        lhs = jnp.concatenate([words[c] for c, _ in picks], axis=1)
-        rhs = jnp.concatenate([tables[t] for _, t in picks], axis=0)
-        spread = jnp.dot(lhs, rhs, preferred_element_type=jnp.float32)
+        spread = None
+        for c, t in picks:
+            term = jnp.dot(words[c], tables[t], preferred_element_type=jnp.float32)
+            spread = term if spread is None else spread + term
         terms = cells.astype(jnp.float32) * spread
         return jnp.sum(terms.reshape(rows // depth, depth, size), axis=0)
 
@@ -110,7 +114,8 @@
     def interior(n, carry):
         b = n + HB
         picks = [
-            (b + HALF + info_s[b, s], info_s[b, nslots + s]) for s in range(nslots)
+            (b + HALF + off_s[s, b], jnp.where(s < cnt_s[0, b], tab_s[s, b], ntab))
+            for s in range(nslots)
         ]
         cols = pl.ds(pl.multiple_of(n * size, size), size)
 
@@ -137,17 +142,33 @@
             copy.start()
         return copies
 
-    sums = to_members(part_in, recv_in, 0)
-
-    out_ref[...] = 0.5 * jnp.dot(
-        cov_ref[...], ctl[...], precision=lax.Precision.HIGHEST, preferred_element_type=jnp.float32
-    )
+    sums = [to_members(part_in, recv_in, 0)]
+
+    chunk = 4 * size
+
+    def static(n, carry):
+        cols = pl.ds(pl.multiple_of(n * chunk, chunk), chunk)
+        for f in range(fields):
+            cov = cov_ref[f, 0:share]
+            for m in range(1, groups):
+                cov = jnp.where(me == m, cov_ref[f, m * share:(m + 1) * share], cov)
+            total = cov[:, 0:1] * ctl[f * levels:f * levels + 1, cols]
+            for l in range(1, levels):
+                at = f * levels + l
+                total = total + cov[:, l:l + 1] * ctl[at:at + 1, cols]
+            out_ref[f, :, cols] = 0.5 * total
+        return carry
+
+    lax.fori_loop(0, nblk * size // chunk, static, 0)
 
     for copy in halo_copies:
         copy.wait()
     sides = [
-        pltpu.make_async_copy(info_halo.at[side], info_side.at[side], side_sem.at[side])
+        pltpu.make_async_copy(src.at[side], dst.at[side], side_sem.at[side, n])
         for side in range(2)
+        for n, (src, dst) in enumerate(
+            [(off_halo, off_side), (tab_halo, tab_side), (cnt_halo, cnt_side)]
+        )
     ]
     for copy in sides:
         copy.start()
@@ -161,7 +182,7 @@
 
     for side in range(2):
         for i in range(HALF):
-            row = 8 - HALF + i if side == 0 else i
+            there = nblk - HALF + i if side == 0 else i
             b = i if side == 0 else nblk + HALF + i
             partners = range(2 * HALF, 2 * HALF + i + 1) if side == 0 else range(
                 b - HB, nblk
@@ -170,8 +191,8 @@
             for c in partners:
                 t = jnp.int32(ntab)
                 for s in range(nslots):
-                    hit = info_side[side, row, s] == c - b
-                    t = jnp.where(hit, info_side[side, row, nslots + s], t)
+                    hit = (off_side[side, s, there] == c - b) & (s < cnt_side[side, 0, there])
+                    t = jnp.where(hit, tab_side[side, s, there], t)
                 picks.append((c, t))
             total = localize(halo[side, i], picks)
 
@@ -195,11 +216,9 @@
             b = n + side * (nblk - HB)
             picks = []
             for s in range(nslots):
-                c = b + HALF + info_s[b, s]
-                held = (c >= 0) & (c < last)
-                picks.append(
-                    (jnp.clip(c, 0, last - 1), jnp.where(held, info_s[b, nslots + s], ntab))
-                )
+                c = b + HALF + off_s[s, b]
+                held = (c >= 0) & (c < last) & (s < cnt_s[0, b])
+                picks.append((jnp.clip(c, 0, last - 1), jnp.where(held, tab_s[s, b], ntab)))
             cols = pl.ds(pl.multiple_of(n * size, size), size)
 
             def dst(m, at, value):
@@ -214,21 +233,23 @@
                 copy.wait()
         near = pl.ds(side * HALF * size, HALF * size)
         part_edge[side, :, :, near] = part_edge[side, :, :, near] + back[side]
-        sums = sums + to_members(part_edge.at[side], recv_edge.at[side], 1 + side)
-
-    for copy in sums:
-        copy.wait()
-
-    def finish(first, width, own_part, others):
+        sums.append(to_members(part_edge.at[side], recv_edge.at[side], 1 + side))
+
+    def finish(copies, first, width, own_part, others):
+        for copy in copies:
+            copy.wait()
         total = own_part
         for d in range(groups - 1):
             total = total + others[d]
         cols = slice(first * size, (first + width) * size)
-        out_ref[:, cols] = out_ref[:, cols] + 0.5 * (total / scale)
-
-    finish(HB, nblk - 2 * HB, part_in[me], recv_in)
+        for f in range(fields):
+            out_ref[f, :, cols] = out_ref[f, :, cols] + 0.5 * (
+                total[f * share:(f + 1) * share] / scale
+            )
+
+    finish(sums[0], HB, nblk - 2 * HB, part_in[me], recv_in)
     for side in range(2):
-        finish(side * (nblk - HB), HB, part_edge[side, me], recv_edge.at[side])
+        finish(sums[1 + side], side * (nblk - HB), HB, part_edge[side, me], recv_edge.at[side])
 
 
 def per_device(perturb, control, static_cov, loc_table, pair_offset, pair_table, pair_count):
@@ -241,29 +262,22 @@
     rows = members * fields * levels
     depth = fields * levels
 
-    live = jnp.arange(nslots, dtype=jnp.int32)[None, :] < pair_count[:, None]
-    info = jnp.concatenate(
-        [jnp.where(live, pair_offset, 0), jnp.where(live, pair_table, ntab)], axis=1
-    )
-    info = jnp.pad(info, ((0, 0), (0, 128 - 2 * nslots)))
-    first = lax.axis_index("member") * share
-    cov_mine = lax.dynamic_slice_in_dim(static_cov, first, share, 1)
-    cov = (cov_mine[:, :, None, :] * jnp.eye(fields, dtype=jnp.float32)[:, None, :, None]).reshape(
-        fields * share, depth
-    )
-
+    offsets = pair_offset.T
+    table_ids = pair_table.T
+    counts = pair_count.reshape(1, nblk)
     out_rows = fields * share
-    f32, bf16 = jnp.float32, jnp.bfloat16
+    f32, bf16, i32 = jnp.float32, jnp.bfloat16, jnp.int32
+    smem = pl.BlockSpec(memory_space=pltpu.SMEM)
     any_spec = pl.BlockSpec(memory_space=pl.ANY)
     dma = pltpu.SemaphoreType.DMA
     pairs = nblk * nslots
-    out = pl.pallas_call(
+    return pl.pallas_call(
         functools.partial(
             kernel, groups, bands, nblk, size, nslots, fields, levels, ntab, members * groups - 1
         ),
-        out_shape=jax.ShapeDtypeStruct((out_rows, width), f32),
+        out_shape=jax.ShapeDtypeStruct((fields, share, width), f32),
         in_specs=[
-            pl.BlockSpec(memory_space=pltpu.SMEM), any_spec, any_spec, any_spec, any_spec,
+            smem, smem, smem, any_spec, any_spec, any_spec, any_spec, any_spec, any_spec,
             pl.BlockSpec(memory_space=pltpu.VMEM),
         ],
         out_specs=pl.BlockSpec(memory_space=pltpu.VMEM),
@@ -274,16 +288,20 @@
             pltpu.VMEM((ntab + 1, size, size), bf16),
             pltpu.VMEM((depth, width), f32),
             pltpu.VMEM((2, depth, HALF * size), f32),
-            pltpu.VMEM((2, 8, 128), jnp.int32),
-            pltpu.SMEM((2, 8, 128), jnp.int32),
+            pltpu.VMEM((2, nslots, nblk), i32),
+            pltpu.VMEM((2, nslots, nblk), i32),
+            pltpu.VMEM((2, 1, nblk), i32),
+            pltpu.SMEM((2, nslots, nblk), i32),
+            pltpu.SMEM((2, nslots, nblk), i32),
+            pltpu.SMEM((2, 1, nblk), i32),
             pltpu.VMEM((groups, out_rows, width - 2 * HB * size), f32),
             pltpu.VMEM((groups - 1, out_rows, width - 2 * HB * size), f32),
             pltpu.VMEM((2, groups, out_rows, HB * size), f32),
             pltpu.VMEM((2, groups - 1, out_rows, HB * size), f32),
             pltpu.VMEM((2, groups, out_rows, HALF * size), f32),
             pltpu.VMEM((2, groups, out_rows, HALF * size), f32),
-            dma((nblk,)), dma((2,)), dma((2,)),
-            dma((2, 2 + HALF)), dma((2, 2 + HALF)),
+            dma((nblk,)), dma((2,)), dma((2, 3)),
+            dma((2, 4 + HALF)), dma((2, 4 + HALF)),
             dma((2,)), dma((2,)),
             dma((3, groups - 1)), dma((3, groups - 1)),
         ],
@@ -293,8 +311,10 @@
         cost_estimate=pl.CostEstimate(
             flops=2 * pairs * rows * size * size, bytes_accessed=2 * rows * width, transcendentals=0
         ),
-    )(info, info, perturb.reshape(rows, width), control.reshape(depth, width), loc_table, cov)
-    return out.reshape(fields, share, width)
+    )(
+        offsets, table_ids, counts, offsets, table_ids, counts,
+        perturb.reshape(rows, width), control.reshape(depth, width), loc_table, static_cov,
+    )
 
 
 def solution(mesh):

time: 61.1 us -> 57.4 us (0.939)
  local copies, waits for them, and re-layouts: 5.28 us -> 1.67 us
  Pallas kernels: 54.4 us -> 55.5 us
  other arithmetic: 0.88 us -> 0 us
    reshape x1 -> x0, local copies, waits for them, and re-layouts: 1.73 us -> none  [per_device(): return out.reshape(fields, share, width)]
    pallas_call x1, Pallas kernels: 54.4 us -> 55.5 us  [per_device(): pl.pallas_call(functools.partial(kernel, groups, bands, nblk, size, nslot...]
    select_n x1 -> x0, other arithmetic: 0.73 us -> none  [per_device(): jnp.where(live, pair_offset, 0)]
    mul x1 -> x0, local copies, waits for them, and re-layouts: 0.67 us -> none  [per_device(): cov_mine[:, :, None, :]]
    pad x1 -> x0, local copies, waits for them, and re-layouts: 0.61 us -> none  [per_device(): info = jnp.pad(info, ((0, 0), (0, 128 - 2 * nslots)))]
    unnamed x4 -> x1, local copies, waits for them, and re-layouts: 2.26 us -> 1.67 us
where the time goes in v2:
time: 57.4 us; the launch traced here: 57.2 us
  Pallas kernels  55.5 us (97%)
  local copies, waits for them, and re-layouts  1.67 us (3%)
    pallas_call x1, Pallas kernels, per_device(): pl.pallas_call(functools.partial(kernel, groups, bands, nblk, size, nslot...  55.5 us
    unnamed x1, local copies, waits for them, and re-layouts  1.67 us

profile of v2, /device:TPU:0, one launch (start us, length us, event | category | flops | bytes accessed | tf_op | source)
XLA Modules:
  0.0 57.2 jit_solution(1783961170160841662)
XLA Ops:
  0.0 55.5 %shard_map.73 = f32[2,4,8192]{2,1,0:T(4,128)} custom-call(s32[12,32]{1,0:T(8,128)} %bitcast.7, s32[12,32]{1,0:T(8,128)} %bitcast.9, s32[1,32]{1,0:T(1,128)} %bitcast.11, s32[12,32]{1,0:T(8,128)} %bitcast.8, s32[12,32]{1,0:T(8,128)} %bitcast.10, s32[1,32]{1,0:T(1,128)} %bitcast.12, bf16[640,8192]{1,0:T(8,128)(2,1)} %bitcast.5, f32[32,8192]{1,0:T(8,128)} %bitcast.6, ...), custom_call_target="tpu_custom_call" | custom-call | flops 32212254720 | bytes 10485760 | tf_op jit(solution)/shard_map/pallas_call | solution.py:274
  55.5 1.7 %copy.9 = f32[2,4,8192]{2,1,0:T(4,128)} copy(f32[2,4,8192]{2,1,0:T(4,128)} %shard_map.73) | data formatting | bytes 524288

commit v3 on v2

--- a/solution.py
+++ b/solution.py
@@ -9,6 +9,7 @@
 
 HB = 6
 HALF = HB // 2
+GROUP = 5
 MESH = pl.DeviceIdType.MESH
 
 
@@ -97,13 +98,21 @@
 
     lax.fori_loop(0, nblk, make_words, 0)
 
+    members = rows // depth
+    group = max(g for g in range(1, GROUP + 1) if members % g == 0)
+
     def localize(cells, picks):
-        spread = None
-        for c, t in picks:
-            term = jnp.dot(words[c], tables[t], preferred_element_type=jnp.float32)
-            spread = term if spread is None else spread + term
-        terms = cells.astype(jnp.float32) * spread
-        return jnp.sum(terms.reshape(rows // depth, depth, size), axis=0)
+        total = None
+        for first in range(0, rows, group * depth):
+            at = pl.ds(first, group * depth)
+            spread = None
+            for c, t in picks:
+                term = jnp.dot(words[c, at], tables[t], preferred_element_type=jnp.float32)
+                spread = term if spread is None else spread + term
+            terms = cells[at].astype(jnp.float32) * spread
+            part = jnp.sum(terms.reshape(group, depth, size), axis=0)
+            total = part if total is None else total + part
+        return total
 
     def put(dst, total):
         for m in range(groups):
@@ -122,7 +131,7 @@
         def dst(m, at, value):
             part_in[m, at, cols] = value
 
-        put(dst, localize(own[b], picks))
+        put(dst, localize(own.at[b], picks))
         return carry
 
     lax.fori_loop(0, nblk - 2 * HB, interior, 0)
@@ -194,7 +203,7 @@
                     hit = (off_side[side, s, there] == c - b) & (s < cnt_side[side, 0, there])
                     t = jnp.where(hit, tab_side[side, s, there], t)
                 picks.append((c, t))
-            total = localize(halo[side, i], picks)
+            total = localize(halo.at[side, i], picks)
 
             def dst(m, at, value):
                 away[side, m, at, i * size:(i + 1) * size] = value
@@ -224,7 +233,7 @@
             def dst(m, at, value):
                 part_edge[side, m, at, cols] = value
 
-            put(dst, localize(own[b], picks))
+            put(dst, localize(own.at[b], picks))
             return carry
 
         lax.fori_loop(0, HB, edge, 0)

time: 57.4 us -> 57.7 us (level)
  no operation moved by 1% of the time
where the time goes in v3:
time: 57.7 us; the launch traced here: 57.5 us
  Pallas kernels  55.8 us (97%)
  local copies, waits for them, and re-layouts  1.67 us (3%)
    pallas_call x1, Pallas kernels, per_device(): pl.pallas_call(functools.partial(kernel, groups, bands, nblk, size, nslot...  55.8 us
    unnamed x1, local copies, waits for them, and re-layouts  1.67 us

profile of v3, /device:TPU:0, one launch (start us, length us, event | category | flops | bytes accessed | tf_op | source)
XLA Modules:
  0.0 57.5 jit_solution(3252525197453549721)
XLA Ops:
  0.0 55.8 %shard_map.73 = f32[2,4,8192]{2,1,0:T(4,128)} custom-call(s32[12,32]{1,0:T(8,128)} %bitcast.7, s32[12,32]{1,0:T(8,128)} %bitcast.9, s32[1,32]{1,0:T(1,128)} %bitcast.11, s32[12,32]{1,0:T(8,128)} %bitcast.8, s32[12,32]{1,0:T(8,128)} %bitcast.10, s32[1,32]{1,0:T(1,128)} %bitcast.12, bf16[640,8192]{1,0:T(8,128)(2,1)} %bitcast.5, f32[32,8192]{1,0:T(8,128)} %bitcast.6, ...), custom_call_target="tpu_custom_call" | custom-call | flops 32212254720 | bytes 10485760 | tf_op jit(solution)/shard_map/pallas_call | solution.py:283
  55.8 1.7 %copy.9 = f32[2,4,8192]{2,1,0:T(4,128)} copy(f32[2,4,8192]{2,1,0:T(4,128)} %shard_map.73) | data formatting | bytes 524288

commit v4 on v3

--- a/solution.py
+++ b/solution.py
@@ -39,6 +39,8 @@
             barrier, inc=1, device_id={"member": lax.rem(me + d, groups)}, device_id_type=MESH
         )
 
+    ends = [*range(HALF), *range(nblk - HALF, nblk)]
+
     def load(b):
         return pltpu.make_async_copy(
             perturb_h.at[:, pl.ds(pl.multiple_of(b * size, size), size)], own.at[b], own_sem.at[b]
@@ -48,37 +50,48 @@
         load(b).start()
         return carry
 
+    for b in ends:
+        load(b).start()
     loads = [
         pltpu.make_async_copy(control_h, ctl, misc_sem.at[0]),
         pltpu.make_async_copy(table_h, tables.at[pl.ds(0, ntab)], misc_sem.at[1]),
     ]
     for copy in loads:
         copy.start()
-    lax.fori_loop(0, nblk, start_load, 0)
+    lax.fori_loop(HALF, nblk - HALF, start_load, 0)
+
+    near = lax.rem(mine + 1, 2)
+    far = 1 - near
+
+    def toward(side):
+        return jnp.where(side == 0, left, right)
+
+    def halo_copies(side):
+        first = jnp.where(side == 0, 0, nblk - HALF)
+        cols = pl.ds(pl.multiple_of(first * size, size), HALF * size)
+        return [
+            pltpu.make_async_remote_copy(
+                src_ref=src, dst_ref=dst.at[1 - side],
+                send_sem=hsend.at[side, n], recv_sem=hrecv.at[1 - side, n],
+                device_id={"band": toward(side)}, device_id_type=MESH,
+            )
+            for n, (src, dst) in enumerate(
+                [
+                    (own.at[pl.ds(first, HALF)], halo),
+                    (control_h.at[:, cols], ctl_halo),
+                    (off_h, off_halo),
+                    (tab_h, tab_halo),
+                    (cnt_h, cnt_halo),
+                ]
+            )
+        ]
+
+    for b in ends:
+        load(b).wait()
     pl.semaphore_wait(barrier, 2 + groups - 1)
-
-    halo_copies = []
-    for side, there, first in ((0, right, nblk - HALF), (1, left, 0)):
-        for n, (src, dst) in enumerate(
-            [
-                (off_h, off_halo.at[side]),
-                (tab_h, tab_halo.at[side]),
-                (cnt_h, cnt_halo.at[side]),
-                (control_h.at[:, pl.ds(first * size, HALF * size)], ctl_halo.at[side]),
-            ]
-            + [
-                (perturb_h.at[:, pl.ds((first + i) * size, size)], halo.at[side, i])
-                for i in range(HALF)
-            ]
-        ):
-            halo_copies.append(
-                pltpu.make_async_remote_copy(
-                    src_ref=src, dst_ref=dst, send_sem=hsend.at[side, n], recv_sem=hrecv.at[side, n],
-                    device_id={"band": there}, device_id_type=MESH,
-                )
-            )
-    for copy in halo_copies:
-        copy.start()
+    for side in (far, near):
+        for copy in halo_copies(side):
+            copy.start()
 
     def word_of(block, weights):
         cells = block.astype(jnp.float32).reshape(rows // depth, depth, size) * weights[None]
@@ -92,11 +105,18 @@
         copy.wait()
 
     def make_words(b, carry):
-        load(b).wait()
         words[b + HALF] = word_of(own[b], ctl[:, pl.ds(pl.multiple_of(b * size, size), size)])
         return carry
 
-    lax.fori_loop(0, nblk, make_words, 0)
+    def end_words(n, carry):
+        return make_words(jnp.where(n < HALF, n, nblk - 2 * HALF + n), carry)
+
+    def loaded_words(b, carry):
+        load(b).wait()
+        return make_words(b, carry)
+
+    lax.fori_loop(0, 2 * HALF, end_words, 0)
+    lax.fori_loop(HALF, nblk - HALF, loaded_words, 0)
 
     members = rows // depth
     group = max(g for g in range(1, GROUP + 1) if members % g == 0)
@@ -170,57 +190,51 @@
 
     lax.fori_loop(0, nblk * size // chunk, static, 0)
 
-    for copy in halo_copies:
-        copy.wait()
-    sides = [
-        pltpu.make_async_copy(src.at[side], dst.at[side], side_sem.at[side, n])
-        for side in range(2)
-        for n, (src, dst) in enumerate(
-            [(off_halo, off_side), (tab_halo, tab_side), (cnt_halo, cnt_side)]
+    def away_copy(side):
+        return pltpu.make_async_remote_copy(
+            src_ref=away.at[side], dst_ref=back.at[1 - side],
+            send_sem=asend.at[side], recv_sem=arecv.at[1 - side],
+            device_id={"band": toward(side)}, device_id_type=MESH,
         )
-    ]
-    for copy in sides:
-        copy.start()
-    for side in range(2):
+
+    for phase, side in enumerate((near, far)):
+        for copy in halo_copies(1 - side):
+            copy.wait_recv()
+        notes = [
+            pltpu.make_async_copy(src.at[side], dst.at[side], side_sem.at[side, n])
+            for n, (src, dst) in enumerate(
+                [(off_halo, off_side), (tab_halo, tab_side), (cnt_halo, cnt_side)]
+            )
+        ]
+        for copy in notes:
+            copy.start()
         for i in range(HALF):
             words[side * (nblk + HALF) + i] = word_of(
                 halo[side, i], ctl_halo[side, :, i * size:(i + 1) * size]
             )
-    for copy in sides:
-        copy.wait()
-
-    for side in range(2):
-        for i in range(HALF):
-            there = nblk - HALF + i if side == 0 else i
-            b = i if side == 0 else nblk + HALF + i
-            partners = range(2 * HALF, 2 * HALF + i + 1) if side == 0 else range(
-                b - HB, nblk
-            )
+        for copy in notes:
+            copy.wait()
+
+        for n in range(HALF):
+            i = jnp.where(side == 0, n, HALF - 1 - n)
+            b = jnp.where(side == 0, i, nblk + HALF + i)
+            there = jnp.where(side == 0, nblk - HALF + i, i)
             picks = []
-            for c in partners:
+            for q in range(n + 1):
+                c = jnp.where(side == 0, 2 * HALF + q, nblk - 1 - q)
                 t = jnp.int32(ntab)
                 for s in range(nslots):
                     hit = (off_side[side, s, there] == c - b) & (s < cnt_side[side, 0, there])
                     t = jnp.where(hit, tab_side[side, s, there], t)
                 picks.append((c, t))
-            total = localize(halo.at[side, i], picks)
+            cols = pl.ds(pl.multiple_of(i * size, size), size)
 
             def dst(m, at, value):
-                away[side, m, at, i * size:(i + 1) * size] = value
-
-            put(dst, total)
-    away_copies = [
-        pltpu.make_async_remote_copy(
-            src_ref=away.at[side], dst_ref=back.at[1 - side],
-            send_sem=asend.at[side], recv_sem=arecv.at[side],
-            device_id={"band": there}, device_id_type=MESH,
-        )
-        for side, there in ((0, left), (1, right))
-    ]
-    for copy in away_copies:
-        copy.start()
-
-    for side in range(2):
+                away[side, m, at, cols] = value
+
+            put(dst, localize(halo.at[side, i], picks))
+        away_copy(side).start()
+
         def edge(n, carry):
             b = n + side * (nblk - HB)
             picks = []
@@ -237,12 +251,15 @@
             return carry
 
         lax.fori_loop(0, HB, edge, 0)
-        if side == 0:
-            for copy in away_copies:
-                copy.wait()
-        near = pl.ds(side * HALF * size, HALF * size)
-        part_edge[side, :, :, near] = part_edge[side, :, :, near] + back[side]
-        sums.append(to_members(part_edge.at[side], recv_edge.at[side], 1 + side))
+        away_copy(1 - side).wait_recv()
+        met = pl.ds(pl.multiple_of(side * HALF * size, size), HALF * size)
+        part_edge[side, :, :, met] = part_edge[side, :, :, met] + back[side]
+        sums.append(to_members(part_edge.at[side], recv_edge.at[side], 1 + phase))
+
+    for side in (near, far):
+        away_copy(side).wait_send()
+        for copy in halo_copies(side):
+            copy.wait_send()
 
     def finish(copies, first, width, own_part, others):
         for copy in copies:
@@ -250,15 +267,15 @@
         total = own_part
         for d in range(groups - 1):
             total = total + others[d]
-        cols = slice(first * size, (first + width) * size)
+        cols = pl.ds(pl.multiple_of(first * size, size), width * size)
         for f in range(fields):
             out_ref[f, :, cols] = out_ref[f, :, cols] + 0.5 * (
                 total[f * share:(f + 1) * share] / scale
             )
 
     finish(sums[0], HB, nblk - 2 * HB, part_in[me], recv_in)
-    for side in range(2):
-        finish(sums[1 + side], side * (nblk - HB), HB, part_edge[side, me], recv_edge.at[side])
+    for phase, side in enumerate((near, far)):
+        finish(sums[1 + phase], side * (nblk - HB), HB, part_edge[side, me], recv_edge.at[side])
 
 
 def per_device(perturb, control, static_cov, loc_table, pair_offset, pair_table, pair_count):
@@ -310,7 +327,7 @@
             pltpu.VMEM((2, groups, out_rows, HALF * size), f32),
             pltpu.VMEM((2, groups, out_rows, HALF * size), f32),
             dma((nblk,)), dma((2,)), dma((2, 3)),
-            dma((2, 4 + HALF)), dma((2, 4 + HALF)),
+            dma((2, 5)), dma((2, 5)),
             dma((2,)), dma((2,)),
             dma((3, groups - 1)), dma((3, groups - 1)),
         ],

time: 57.7 us -> 58.4 us (1.012)
  Pallas kernels: 55.8 us -> 56.5 us
    pallas_call x1, Pallas kernels: 55.8 us -> 56.5 us  [per_device(): pl.pallas_call(functools.partial(kernel, groups, bands, nblk, size, nslot...]
where the time goes in v4:
time: 58.4 us; the launch traced here: 58.2 us
  Pallas kernels  56.5 us (97%)
  local copies, waits for them, and re-layouts  1.67 us (3%)
    pallas_call x1, Pallas kernels, per_device(): pl.pallas_call(functools.partial(kernel, groups, bands, nblk, size, nslot...  56.5 us
    unnamed x1, local copies, waits for them, and re-layouts  1.67 us

profile of v4, /device:TPU:0, one launch (start us, length us, event | category | flops | bytes accessed | tf_op | source)
XLA Modules:
  0.0 58.2 jit_solution(8173454426243009881)
XLA Ops:
  0.0 56.5 %shard_map.73 = f32[2,4,8192]{2,1,0:T(4,128)} custom-call(s32[12,32]{1,0:T(8,128)} %bitcast.7, s32[12,32]{1,0:T(8,128)} %bitcast.9, s32[1,32]{1,0:T(1,128)} %bitcast.11, s32[12,32]{1,0:T(8,128)} %bitcast.8, s32[12,32]{1,0:T(8,128)} %bitcast.10, s32[1,32]{1,0:T(1,128)} %bitcast.12, bf16[640,8192]{1,0:T(8,128)(2,1)} %bitcast.5, f32[32,8192]{1,0:T(8,128)} %bitcast.6, ...), custom_call_target="tpu_custom_call" | custom-call | flops 32212254720 | bytes 10485760 | tf_op jit(solution)/shard_map/pallas_call | solution.py:300
  56.5 1.7 %copy.9 = f32[2,4,8192]{2,1,0:T(4,128)} copy(f32[2,4,8192]{2,1,0:T(4,128)} %shard_map.73) | data formatting | bytes 524288

commit v5 on v3

--- a/solution.py
+++ b/solution.py
@@ -96,7 +96,7 @@
         words[b + HALF] = word_of(own[b], ctl[:, pl.ds(pl.multiple_of(b * size, size), size)])
         return carry
 
-    lax.fori_loop(0, nblk, make_words, 0)
+    lax.fori_loop(0, 2 * HB + 2, make_words, 0)
 
     members = rows // depth
     group = max(g for g in range(1, GROUP + 1) if members % g == 0)
@@ -134,7 +134,18 @@
         put(dst, localize(own.at[b], picks))
         return carry
 
-    lax.fori_loop(0, nblk - 2 * HB, interior, 0)
+    def two(n, carry):
+        interior(2 * n, carry)
+        return interior(2 * n + 1, carry)
+
+    def two_and_words(n, carry):
+        two(n, carry)
+        make_words(2 * n + 2 * HB + 2, carry)
+        return make_words(2 * n + 2 * HB + 3, carry)
+
+    steps = (nblk - 2 * HB) // 2
+    lax.fori_loop(0, steps - 1, two_and_words, 0)
+    two(steps - 1, 0)
 
     def to_members(src, dst, n):
         copies = []
@@ -236,7 +247,11 @@
             put(dst, localize(own.at[b], picks))
             return carry
 
-        lax.fori_loop(0, HB, edge, 0)
+        def two_edges(n, carry):
+            edge(2 * n, carry)
+            return edge(2 * n + 1, carry)
+
+        lax.fori_loop(0, HB // 2, two_edges, 0)
         if side == 0:
             for copy in away_copies:
                 copy.wait()

time: 57.7 us -> 54.4 us (0.943)
  Pallas kernels: 55.8 us -> 52.5 us
    pallas_call x1, Pallas kernels: 55.8 us -> 52.5 us  [per_device(): pl.pallas_call(functools.partial(kernel, groups, bands, nblk, size, nslot...]
where the time goes in v5:
time: 54.4 us; the launch traced here: 54.2 us
  Pallas kernels  52.5 us (97%)
  local copies, waits for them, and re-layouts  1.67 us (3%)
    pallas_call x1, Pallas kernels, per_device(): pl.pallas_call(functools.partial(kernel, groups, bands, nblk, size, nslot...  52.5 us
    unnamed x1, local copies, waits for them, and re-layouts  1.67 us

profile of v5, /device:TPU:0, one launch (start us, length us, event | category | flops | bytes accessed | tf_op | source)
XLA Modules:
  0.0 54.2 jit_solution(4080900953512023673)
XLA Ops:
  0.0 52.5 %shard_map.73 = f32[2,4,8192]{2,1,0:T(4,128)} custom-call(s32[12,32]{1,0:T(8,128)} %bitcast.7, s32[12,32]{1,0:T(8,128)} %bitcast.9, s32[1,32]{1,0:T(1,128)} %bitcast.11, s32[12,32]{1,0:T(8,128)} %bitcast.8, s32[12,32]{1,0:T(8,128)} %bitcast.10, s32[1,32]{1,0:T(1,128)} %bitcast.12, bf16[640,8192]{1,0:T(8,128)(2,1)} %bitcast.5, f32[32,8192]{1,0:T(8,128)} %bitcast.6, ...), custom_call_target="tpu_custom_call" | custom-call | flops 32212254720 | bytes 10485760 | tf_op jit(solution)/shard_map/pallas_call | solution.py:298
  52.6 1.7 %copy.9 = f32[2,4,8192]{2,1,0:T(4,128)} copy(f32[2,4,8192]{2,1,0:T(4,128)} %shard_map.73) | data formatting | bytes 524288
